TPU v7x, 32 devices: a whole 2x2x4 slice. The times are simulated.
32 devices in a mesh: split: 8 (over y, x, core), shard: 4 (over z).
Axes of the slice: x: 2, y: 2, z: 4, core: 2. Of those that a mesh axis runs over, the one named last changes fastest.
Arguments:
- strain: bfloat16 [3, 4096], P(None, ('split', 'shard')), may hold values from -6 to 6
- basis: bfloat16 [8, 400, 2048], P('split', 'shard'), may hold values from -0.125 to 0.125
- recon: bfloat16 [8, 2, 2048, 400], P('split', None, 'shard'), may hold values from -0.3125 to 0.3125
Outputs:
- snr2: float32 [8, 2048, 2048], P('split', 'shard')
- loudest: float32 [2048], replicated
All inputs are finite; a program needn't handle non-finite values.
Results may differ from a plain program's by a relative error of at most 0.0025.
Values may be sent and summed in bfloat16 or wider, within the bound.
A program may use at most 128 MiB of HBM per device.

v0:
```python
import functools

import jax
import jax.numpy as jnp
from jax import lax
from jax.experimental import pallas as pl
from jax.experimental.pallas import tpu as pltpu
from jax.sharding import PartitionSpec as P

MESH = pl.DeviceIdType.MESH
LANES = 128


def kernel(
    nsplit, nshard, nb, pad, chunks, ntile, scale,
    strain_ref, basis_ref, recon_ref,
    snr_ref, loud_ref,
    parts, rows, tiles, held, acc, series, weights, localmax, splitmax, shardmax,
    strain_send, strain_recv, wide_send, wide_recv,
    basis_send, basis_recv, smax_send, smax_recv, hmax_send, hmax_recv,
):
    split = lax.axis_index("split")
    shard = lax.axis_index("shard")
    ndet, width = strain_ref.shape
    taps = basis_ref.shape[1]
    tout = snr_ref.shape[1]
    templ = snr_ref.shape[0]
    ctaps = taps // chunks
    ktiles = taps // LANES
    nrows = (taps + tout) // LANES

    barrier = pltpu.get_barrier_semaphore()
    for off in range(1, nshard):
        pl.semaphore_signal(barrier, inc=1, device_id={"shard": lax.rem(shard + off, nshard)}, device_id_type=MESH)
    for off in range(1, nsplit):
        pl.semaphore_signal(barrier, inc=1, device_id={"split": lax.rem(split + off, nsplit)}, device_id_type=MESH)
    pl.semaphore_wait(barrier, nshard + nsplit - 2)

    parts[split, shard, :ndet] = strain_ref[...].astype(jnp.float32)

    def strain_copy(off):
        return pltpu.make_async_remote_copy(
            src_ref=parts.at[split, shard], dst_ref=parts.at[split, shard],
            send_sem=strain_send.at[off - 1], recv_sem=strain_recv.at[off - 1],
            device_id={"shard": lax.rem(shard + off, nshard)}, device_id_type=MESH)

    def wide_copy(off):
        return pltpu.make_async_remote_copy(
            src_ref=parts.at[split], dst_ref=parts.at[split],
            send_sem=wide_send.at[off - 1], recv_sem=wide_recv.at[off - 1],
            device_id={"split": lax.rem(split + off, nsplit)}, device_id_type=MESH)

    for off in range(1, nshard):
        strain_copy(off).start()

    def chunk_of(ref, chunk):
        return ref.at[:, pl.ds(pl.multiple_of(chunk * ctaps, ctaps), ctaps)]

    def basis_copy(way, block, chunk, own):
        dst = chunk_of(held.at[block], chunk)
        src = chunk_of(basis_ref, chunk) if own else dst
        target = shard + 1 if way == 0 else shard - 1
        return pltpu.make_async_remote_copy(
            src_ref=src, dst_ref=dst,
            send_sem=basis_send.at[way, block, chunk], recv_sem=basis_recv.at[block, chunk],
            device_id={"shard": target}, device_id_type=MESH)

    for chunk in range(chunks):
        @pl.when(shard < nshard - 1)
        def _():
            basis_copy(0, shard, chunk, True).start()

        @pl.when(shard > 0)
        def _():
            basis_copy(1, shard, chunk, True).start()

    lrow = lax.broadcasted_iota(jnp.int32, (nb * nshard, pad * nshard), 0)
    lcol = lax.broadcasted_iota(jnp.int32, (nb * nshard, pad * nshard), 1)
    within = lax.rem(lcol, pad)
    chosen = (lrow == (lcol - within) // pad * nb + within) & (within < nb)
    select = jnp.where(chosen, 1.0, 0.0).astype(jnp.bfloat16)

    @pl.loop(0, 2 * templ // 256)
    def _(part):
        at = pl.ds(pl.multiple_of(part * 256, 256), 256)
        weights[at, :] = jnp.dot(recon_ref[at, :], select, preferred_element_type=jnp.float32).astype(jnp.bfloat16)

    for off in range(1, nshard):
        strain_copy(off).wait_recv()
    for off in range(1, nsplit):
        wide_copy(off).start()

    @pl.loop(0, ndet * nshard * pad // 64)
    def _(part):
        per = nshard * pad // 64
        series[part // per, pl.ds(pl.multiple_of(lax.rem(part, per) * 64, 64), 64), :] = jnp.zeros((64, tout), jnp.bfloat16)

    for off in range(1, nsplit):
        wide_copy(off).wait_recv()

    per = LANES // width
    if per > 1:
        for piece in range(nsplit * nshard):
            rows[piece // per, :, (piece % per) * width : (piece % per + 1) * width] = parts[piece // nshard, piece % nshard]

    def rolled(b):
        if per > 1:
            block = rows[b]
        else:
            block = parts[b // nshard, lax.rem(b, nshard)]
        return tuple(
            pltpu.roll(jnp.broadcast_to(block[d : d + 1, :], (LANES, LANES)), 1, 1, stride=1, stride_axis=0)
            for d in range(ndet))

    above = lax.broadcasted_iota(jnp.int32, (LANES, LANES), 1) > lax.broadcasted_iota(jnp.int32, (LANES, LANES), 0)

    def tile_step(b, last):
        now = rolled(b)
        at = pl.ds(pl.multiple_of((b - 1) * LANES, LANES), LANES)
        for d in range(ndet):
            tiles[d, :, at] = jnp.where(above, now[d], last[d]).astype(jnp.bfloat16)
        return now

    lax.fori_loop(1, nrows, tile_step, rolled(jnp.int32(0)))

    def fir(filters, slot, block, chunk):
        per_det = tout // ntile

        @pl.loop(0, ndet * per_det)
        def _(step):
            det = step // per_det
            begin = lax.rem(step, per_det) * ntile
            frame = jnp.concatenate([
                tiles[det, :, pl.ds(pl.multiple_of(begin + (ktiles - 1 - i) * LANES - chunk * ctaps, LANES), ntile)]
                for i in range(ctaps // LANES)], axis=0)
            at = pl.ds(pl.multiple_of(begin, ntile), ntile)
            total = jnp.dot(filters[...], frame, preferred_element_type=jnp.float32)
            total = jnp.where(chunk > 0, acc[slot, det, :, at], 0.0) + total
            acc[slot, det, :, at] = total
            series[det, pl.ds(pl.multiple_of(block * pad, pad), nb), at] = total.astype(jnp.bfloat16)

    ahead = min(2, chunks)

    @pl.loop(0, ahead)
    def _(chunk):
        fir(chunk_of(basis_ref, chunk), 2, shard, chunk)

    @pl.loop(0, (nshard - 1) * chunks)
    def _(step):
        hop, chunk = step // chunks, lax.rem(step, chunks)
        below, over = shard - 1 - hop, shard + 1 + hop

        @pl.when(below >= 0)
        def _():
            basis_copy(0, below, chunk, False).wait_recv()

            @pl.when(shard < nshard - 1)
            def _():
                basis_copy(0, below, chunk, False).start()

        @pl.when(over < nshard)
        def _():
            basis_copy(1, over, chunk, False).wait_recv()

            @pl.when(shard > 0)
            def _():
                basis_copy(1, over, chunk, False).start()

        @pl.when(step + ahead < chunks)
        def _():
            fir(chunk_of(basis_ref, step + ahead), 2, shard, step + ahead)

        @pl.when(below >= 0)
        def _():
            fir(chunk_of(held.at[below], chunk), 0, below, chunk)

        @pl.when(over < nshard)
        def _():
            fir(chunk_of(held.at[over], chunk), 1, over, chunk)

    rtile = 256

    @pl.loop(0, tout // rtile)
    def _(step):
        at = pl.ds(pl.multiple_of(step * rtile, rtile), rtile)
        total = None
        for det in range(ndet):
            z = jnp.dot(weights[...], series[det, :, at], preferred_element_type=jnp.float32)
            z = z * z
            z = z[:templ] + z[templ:]
            total = z if total is None else total + z
        total = total * scale
        snr_ref[:, at] = total
        top = jnp.max(total, axis=0, keepdims=True)
        for i in range(rtile // LANES):
            localmax[pl.ds(step * (rtile // LANES) + i, 1), :] = top[:, i * LANES : (i + 1) * LANES]

    def smax_copy(off):
        return pltpu.make_async_remote_copy(
            src_ref=localmax, dst_ref=splitmax.at[off - 1],
            send_sem=smax_send.at[off - 1], recv_sem=smax_recv.at[off - 1],
            device_id={"split": lax.rem(split + off, nsplit)}, device_id_type=MESH)

    for off in range(1, nsplit):
        smax_copy(off).start()
    for off in range(1, nsplit):
        smax_copy(off).wait_recv()
    most = localmax[...]
    for off in range(1, nsplit):
        most = jnp.maximum(most, splitmax[off - 1])
    shardmax[nshard - 1] = most

    def hmax_copy(off):
        return pltpu.make_async_remote_copy(
            src_ref=shardmax.at[nshard - 1], dst_ref=shardmax.at[off - 1],
            send_sem=hmax_send.at[off - 1], recv_sem=hmax_recv.at[off - 1],
            device_id={"shard": lax.rem(shard + off, nshard)}, device_id_type=MESH)

    for off in range(1, nshard):
        hmax_copy(off).start()
    for off in range(1, nshard):
        hmax_copy(off).wait_recv()
    for off in range(1, nshard):
        most = jnp.maximum(most, shardmax[off - 1])
    loud_ref[...] = most

    for off in range(1, nshard):
        strain_copy(off).wait_send()
        hmax_copy(off).wait_send()
    for off in range(1, nsplit):
        wide_copy(off).wait_send()
        smax_copy(off).wait_send()

    @pl.loop(0, nshard * chunks)
    def _(step):
        block, chunk = step // chunks, lax.rem(step, chunks)

        @pl.when((block <= shard) & (shard < nshard - 1))
        def _():
            basis_copy(0, block, chunk, False).wait_send()

        @pl.when((block >= shard) & (shard > 0))
        def _():
            basis_copy(1, block, chunk, False).wait_send()


def per_device(nsplit, nshard, strain, basis, recon):
    ndet, width = strain.shape
    _, nb, taps = basis.shape
    _, _, templ, nbasis = recon.shape
    tout = width * nsplit * nshard - taps
    pad = -(-nb // 64) * 64
    chunks = 4
    ntile = 512
    vmem = pl.BlockSpec(memory_space=pltpu.VMEM)
    dma = pltpu.SemaphoreType.DMA
    snr, loud = pl.pallas_call(
        functools.partial(kernel, nsplit, nshard, nb, pad, chunks, ntile, 1.0 / (2.0 * ndet)),
        out_shape=(
            jax.ShapeDtypeStruct((templ, tout), jnp.float32),
            jax.ShapeDtypeStruct((tout // LANES, LANES), jnp.float32),
        ),
        in_specs=[vmem] * 3,
        out_specs=(vmem, vmem),
        scratch_shapes=[
            pltpu.VMEM((nsplit, nshard, 8, width), jnp.float32),
            pltpu.VMEM(((taps + tout) // LANES, 8, LANES), jnp.float32),
            pltpu.VMEM((ndet, LANES, taps + tout - LANES), jnp.bfloat16),
            pltpu.VMEM((nshard, nb, taps), jnp.bfloat16),
            pltpu.VMEM((3, ndet, nb, tout), jnp.float32),
            pltpu.VMEM((ndet, nshard * pad, tout), jnp.bfloat16),
            pltpu.VMEM((2 * templ, nshard * pad), jnp.bfloat16),
            pltpu.VMEM((tout // LANES, LANES), jnp.float32),
            pltpu.VMEM((nsplit - 1, tout // LANES, LANES), jnp.float32),
            pltpu.VMEM((nshard, tout // LANES, LANES), jnp.float32),
            dma((nshard - 1,)), dma((nshard - 1,)),
            dma((nsplit - 1,)), dma((nsplit - 1,)),
            dma((2, nshard, chunks)), dma((nshard, chunks)),
            dma((nsplit - 1,)), dma((nsplit - 1,)),
            dma((nshard - 1,)), dma((nshard - 1,)),
        ],
        compiler_params=pltpu.CompilerParams(
            collective_id=0, has_side_effects=True, vmem_limit_bytes=56 * 1024 * 1024),
    )(strain, basis[0], recon[0].reshape(2 * templ, nbasis))
    return snr[None], loud.reshape(tout)


def solution(mesh):
    return jax.shard_map(
        functools.partial(per_device, mesh.shape["split"], mesh.shape["shard"]),
        mesh=mesh,
        in_specs=(
            P(None, ("split", "shard")),
            P("split", "shard", None),
            P("split", None, "shard", None),
        ),
        out_specs=(P("split", "shard", None), P()),
        check_vma=False,
    )
```

profile of v0, /device:TPU:0, one launch (start us, length us, event | category | flops | bytes accessed | tf_op | source)
XLA Modules:
  0.0 93.3 jit_solution(1541642565767374140)
XLA Ops:
  0.6 2.2 %copy.5 = bf16[1,2,512,400]{3,2,1,0:T(8,128)(2,1)} copy(bf16[1,2,512,400]{2,3,1,0:T(8,128)(2,1)} %param.5) | data formatting | bytes 1638400 | tf_op args[2]
  2.9 85.1 %shard_map.50 = (f32[512,2048]{1,0:T(8,128)}, f32[16,128]{1,0:T(8,128)}) custom-call(bf16[3,128]{1,0:T(4,128)(2,1)} %strain_ref.1, bf16[100,2048]{1,0:T(8,128)(2,1)} %bitcast.6, bf16[1024,400]{1,0:T(8,128)(2,1)} %bitcast.4), custom_call_target="tpu_custom_call" | custom-call | tf_op jit(solution)/shard_map/pallas_call | solution.py:257
  87.9 0.0 copy-start
  88.0 4.7 %copy.8 = f32[1,512,2048]{2,1,0:T(8,128)} copy(f32[1,512,2048]{2,1,0:T(8,128)} %bitcast.5) | data formatting | bytes 8388608
  92.7 0.0 copy-done
  92.7 0.6 copy.9
Async XLA Ops:
  87.9 4.7 %copy-start = (f32[16,128]{1,0:T(8,128)S(1)}, f32[16,128]{1,0:T(8,128)}, u32[]{:S(2)}) copy-start(f32[16,128]{1,0:T(8,128)} %get-tuple-element.5) | copy-start | bytes 24580
where the time goes:
time: 93.4 us; the launch traced here: 93.3 us
  Pallas kernels  85.1 us (91%)
  local copies, waits for them, and re-layouts  7.54 us (8%)
    pallas_call x1, Pallas kernels, per_device(): pl.pallas_call(functools.partial(kernel, nsplit, nshard, nb, pad, chunks,...  85.1 us
    unnamed x5, local copies, waits for them, and re-layouts  7.54 us

commit v1 on v0

--- a/solution.py
+++ b/solution.py
@@ -12,10 +12,10 @@
 
 
 def kernel(
-    nsplit, nshard, nb, pad, chunks, ntile, scale,
+    nsplit, nshard, nb, pad, chunks, mtile, scale,
     strain_ref, basis_ref, recon_ref,
     snr_ref, loud_ref,
-    parts, rows, tiles, held, acc, series, weights, localmax, splitmax, shardmax,
+    parts, rows, tiles, held, pair, acc, series, weights, localmax, splitmax, shardmax,
     strain_send, strain_recv, wide_send, wide_recv,
     basis_send, basis_recv, smax_send, smax_recv, hmax_send, hmax_recv,
 ):
@@ -36,6 +36,7 @@
         pl.semaphore_signal(barrier, inc=1, device_id={"split": lax.rem(split + off, nsplit)}, device_id_type=MESH)
     pl.semaphore_wait(barrier, nshard + nsplit - 2)
 
+    parts[split, shard] = jnp.zeros((8, width), jnp.float32)
     parts[split, shard, :ndet] = strain_ref[...].astype(jnp.float32)
 
     def strain_copy(off):
@@ -74,26 +75,26 @@
         def _():
             basis_copy(1, shard, chunk, True).start()
 
+    held[shard] = basis_ref[...]
     lrow = lax.broadcasted_iota(jnp.int32, (nb * nshard, pad * nshard), 0)
     lcol = lax.broadcasted_iota(jnp.int32, (nb * nshard, pad * nshard), 1)
     within = lax.rem(lcol, pad)
     chosen = (lrow == (lcol - within) // pad * nb + within) & (within < nb)
     select = jnp.where(chosen, 1.0, 0.0).astype(jnp.bfloat16)
-
-    @pl.loop(0, 2 * templ // 256)
-    def _(part):
-        at = pl.ds(pl.multiple_of(part * 256, 256), 256)
-        weights[at, :] = jnp.dot(recon_ref[at, :], select, preferred_element_type=jnp.float32).astype(jnp.bfloat16)
+    for q in range(2):
+        @pl.loop(0, templ // 256)
+        def _(part):
+            begin = pl.multiple_of(part * 256, 256)
+            placed = lax.dot_general(
+                recon_ref[q, :, pl.ds(begin, 256)], select, (((0,), (0,)), ((), ())),
+                preferred_element_type=jnp.float32)
+            weights[pl.ds(pl.multiple_of(q * templ + begin, 256), 256), :] = placed.astype(jnp.bfloat16)
+    pair[...] = jnp.zeros_like(pair)
 
     for off in range(1, nshard):
         strain_copy(off).wait_recv()
     for off in range(1, nsplit):
         wide_copy(off).start()
-
-    @pl.loop(0, ndet * nshard * pad // 64)
-    def _(part):
-        per = nshard * pad // 64
-        series[part // per, pl.ds(pl.multiple_of(lax.rem(part, per) * 64, 64), 64), :] = jnp.zeros((64, tout), jnp.bfloat16)
 
     for off in range(1, nsplit):
         wide_copy(off).wait_recv()
@@ -118,32 +119,39 @@
         now = rolled(b)
         at = pl.ds(pl.multiple_of((b - 1) * LANES, LANES), LANES)
         for d in range(ndet):
-            tiles[d, :, at] = jnp.where(above, now[d], last[d]).astype(jnp.bfloat16)
+            tiles[d, at, :] = jnp.where(above, now[d], last[d]).T.astype(jnp.bfloat16)
         return now
 
     lax.fori_loop(1, nrows, tile_step, rolled(jnp.int32(0)))
 
-    def fir(filters, slot, block, chunk):
-        per_det = tout // ntile
+    def fir(first, second, chunk):
+        at_taps = pl.ds(pl.multiple_of(chunk * ctaps, ctaps), ctaps)
+        pair[:nb, :] = held[first, :, at_taps]
+        pair[pad : pad + nb, :] = held[second, :, at_taps]
+        per_det = tout // mtile
 
         @pl.loop(0, ndet * per_det)
         def _(step):
             det = step // per_det
-            begin = lax.rem(step, per_det) * ntile
+            begin = lax.rem(step, per_det) * mtile
             frame = jnp.concatenate([
-                tiles[det, :, pl.ds(pl.multiple_of(begin + (ktiles - 1 - i) * LANES - chunk * ctaps, LANES), ntile)]
-                for i in range(ctaps // LANES)], axis=0)
-            at = pl.ds(pl.multiple_of(begin, ntile), ntile)
-            total = jnp.dot(filters[...], frame, preferred_element_type=jnp.float32)
-            total = jnp.where(chunk > 0, acc[slot, det, :, at], 0.0) + total
-            acc[slot, det, :, at] = total
-            series[det, pl.ds(pl.multiple_of(block * pad, pad), nb), at] = total.astype(jnp.bfloat16)
-
-    ahead = min(2, chunks)
-
-    @pl.loop(0, ahead)
-    def _(chunk):
-        fir(chunk_of(basis_ref, chunk), 2, shard, chunk)
+                tiles[det, pl.ds(pl.multiple_of(begin + (ktiles - 1 - i) * LANES - chunk * ctaps, LANES), mtile), :]
+                for i in range(ctaps // LANES)], axis=1)
+            at = pl.ds(pl.multiple_of(begin, mtile), mtile)
+            total = lax.dot_general(frame, pair[...], (((1,), (1,)), ((), ())), preferred_element_type=jnp.float32)
+            total = jnp.where(chunk > 0, acc[det, at, :], 0.0) + total
+            acc[det, at, :] = total
+
+            @pl.when(chunk == chunks - 1)
+            def _():
+                series[det, at, pl.ds(pl.multiple_of(first * pad, pad), pad)] = total[:, :pad].astype(jnp.bfloat16)
+                series[det, at, pl.ds(pl.multiple_of(second * pad, pad), pad)] = total[:, pad:].astype(jnp.bfloat16)
+
+    both = jnp.minimum(shard, nshard - 1 - shard)
+    upper = shard >= nshard // 2
+
+    def single(hop):
+        return jnp.where(upper, shard - 1 - hop, shard + 1 + hop)
 
     @pl.loop(0, (nshard - 1) * chunks)
     def _(step):
@@ -166,17 +174,13 @@
             def _():
                 basis_copy(1, over, chunk, False).start()
 
-        @pl.when(step + ahead < chunks)
-        def _():
-            fir(chunk_of(basis_ref, step + ahead), 2, shard, step + ahead)
-
-        @pl.when(below >= 0)
-        def _():
-            fir(chunk_of(held.at[below], chunk), 0, below, chunk)
-
-        @pl.when(over < nshard)
-        def _():
-            fir(chunk_of(held.at[over], chunk), 1, over, chunk)
+        late = hop - both
+
+        @pl.when((late < 0) | ((late < nshard - 1 - 2 * both) & (lax.rem(late + 2 * nshard, 2) == 0)))
+        def _():
+            first = jnp.where(late < 0, below, jnp.where(late == 0, shard, single(hop - 1)))
+            second = jnp.where(late < 0, over, single(hop))
+            fir(first, second, chunk)
 
     rtile = 256
 
@@ -185,7 +189,8 @@
         at = pl.ds(pl.multiple_of(step * rtile, rtile), rtile)
         total = None
         for det in range(ndet):
-            z = jnp.dot(weights[...], series[det, :, at], preferred_element_type=jnp.float32)
+            z = lax.dot_general(
+                weights[...], series[det, at, :], (((1,), (1,)), ((), ())), preferred_element_type=jnp.float32)
             z = z * z
             z = z[:templ] + z[templ:]
             total = z if total is None else total + z
@@ -247,17 +252,17 @@
 def per_device(nsplit, nshard, strain, basis, recon):
     ndet, width = strain.shape
     _, nb, taps = basis.shape
-    _, _, templ, nbasis = recon.shape
+    templ = recon.shape[2]
     tout = width * nsplit * nshard - taps
-    pad = -(-nb // 64) * 64
+    pad = -(-nb // LANES) * LANES
     chunks = 4
-    ntile = 512
+    mtile = 1024
     vmem = pl.BlockSpec(memory_space=pltpu.VMEM)
     dma = pltpu.SemaphoreType.DMA
     snr, loud = pl.pallas_call(
-        functools.partial(kernel, nsplit, nshard, nb, pad, chunks, ntile, 1.0 / (2.0 * ndet)),
+        functools.partial(kernel, nsplit, nshard, nb, pad, chunks, mtile, 1.0 / (2.0 * ndet)),
         out_shape=(
-            jax.ShapeDtypeStruct((templ, tout), jnp.float32),
+            pltpu.VMEM((templ, tout), jnp.float32),
             jax.ShapeDtypeStruct((tout // LANES, LANES), jnp.float32),
         ),
         in_specs=[vmem] * 3,
@@ -265,10 +270,11 @@
         scratch_shapes=[
             pltpu.VMEM((nsplit, nshard, 8, width), jnp.float32),
             pltpu.VMEM(((taps + tout) // LANES, 8, LANES), jnp.float32),
-            pltpu.VMEM((ndet, LANES, taps + tout - LANES), jnp.bfloat16),
+            pltpu.VMEM((ndet, taps + tout - LANES, LANES), jnp.bfloat16),
             pltpu.VMEM((nshard, nb, taps), jnp.bfloat16),
-            pltpu.VMEM((3, ndet, nb, tout), jnp.float32),
-            pltpu.VMEM((ndet, nshard * pad, tout), jnp.bfloat16),
+            pltpu.VMEM((2 * pad, taps // chunks), jnp.bfloat16),
+            pltpu.VMEM((ndet, tout, 2 * pad), jnp.float32),
+            pltpu.VMEM((ndet, tout, nshard * pad), jnp.bfloat16),
             pltpu.VMEM((2 * templ, nshard * pad), jnp.bfloat16),
             pltpu.VMEM((tout // LANES, LANES), jnp.float32),
             pltpu.VMEM((nsplit - 1, tout // LANES, LANES), jnp.float32),
@@ -281,7 +287,7 @@
         ],
         compiler_params=pltpu.CompilerParams(
             collective_id=0, has_side_effects=True, vmem_limit_bytes=56 * 1024 * 1024),
-    )(strain, basis[0], recon[0].reshape(2 * templ, nbasis))
+    )(strain, basis[0], jnp.swapaxes(recon[0], 1, 2))
     return snr[None], loud.reshape(tout)
 
 

time: 93.4 us -> 67.8 us (0.73)
  Pallas kernels: 85.1 us -> 64.4 us
  local copies, waits for them, and re-layouts: 7.54 us -> 2.62 us
    pallas_call x1, Pallas kernels: 85.1 us -> 64.4 us  [per_device(): pl.pallas_call(functools.partial(kernel, nsplit, nshard, nb, pad, chunks,...]
    unnamed x5 -> x4, local copies, waits for them, and re-layouts: 7.54 us -> 2.62 us
where the time goes in v1:
time: 67.8 us; the launch traced here: 67.7 us
  Pallas kernels  64.4 us (95%)
  local copies, waits for them, and re-layouts  2.62 us (4%)
    pallas_call x1, Pallas kernels, per_device(): pl.pallas_call(functools.partial(kernel, nsplit, nshard, nb, pad, chunks,...  64.4 us
    unnamed x4, local copies, waits for them, and re-layouts  2.62 us

profile of v1, /device:TPU:0, one launch (start us, length us, event | category | flops | bytes accessed | tf_op | source)
XLA Modules:
  0.0 67.7 jit_solution(17821007462984047652)
XLA Ops:
  0.6 64.4 %shard_map.50 = (f32[512,2048]{1,0:T(8,128)S(1)}, f32[16,128]{1,0:T(8,128)}) custom-call(bf16[3,128]{1,0:T(4,128)(2,1)} %strain_ref.1, bf16[100,2048]{1,0:T(8,128)(2,1)} %bitcast.8, bf16[2,400,512]{2,1,0:T(8,128)(2,1)} %bitcast.7), custom_call_target="tpu_custom_call" | custom-call | tf_op jit(solution)/shard_map/pallas_call | solution.py:262
  65.1 0.0 copy-start
  65.1 2.0 %copy.7 = f32[1,512,2048]{2,1,0:T(8,128)} copy(f32[1,512,2048]{2,1,0:T(8,128)S(1)} %bitcast.6) | data formatting | bytes 8388608
  67.1 0.0 copy-done
  67.1 0.6 copy.8
Async XLA Ops:
  65.1 2.0 %copy-start = (f32[16,128]{1,0:T(8,128)S(1)}, f32[16,128]{1,0:T(8,128)}, u32[]{:S(2)}) copy-start(f32[16,128]{1,0:T(8,128)} %get-tuple-element.5) | copy-start | bytes 24580

commit v2 on v1

--- a/solution.py
+++ b/solution.py
@@ -99,6 +99,36 @@
     for off in range(1, nsplit):
         wide_copy(off).wait_recv()
 
+    steps = (nshard - 1) * chunks
+    middle = (shard > 0) & (shard < nshard - 1)
+    ahead = chunks - 1
+    lead = jnp.where(middle, ahead, 0)
+
+    def advance(step):
+        hop, chunk = step // chunks, lax.rem(step, chunks)
+        below, over = shard - 1 - hop, shard + 1 + hop
+
+        @pl.when(below >= 0)
+        def _():
+            basis_copy(0, below, chunk, False).wait_recv()
+
+            @pl.when(shard < nshard - 1)
+            def _():
+                basis_copy(0, below, chunk, False).start()
+
+        @pl.when(over < nshard)
+        def _():
+            basis_copy(1, over, chunk, False).wait_recv()
+
+            @pl.when(shard > 0)
+            def _():
+                basis_copy(1, over, chunk, False).start()
+
+    @pl.when(middle)
+    def _():
+        for step in range(ahead - 1):
+            advance(jnp.int32(step))
+
     per = LANES // width
     if per > 1:
         for piece in range(nsplit * nshard):
@@ -123,6 +153,10 @@
         return now
 
     lax.fori_loop(1, nrows, tile_step, rolled(jnp.int32(0)))
+
+    @pl.when(middle)
+    def _():
+        advance(jnp.int32(ahead - 1))
 
     def fir(first, second, chunk):
         at_taps = pl.ds(pl.multiple_of(chunk * ctaps, ctaps), ctaps)
@@ -153,27 +187,14 @@
     def single(hop):
         return jnp.where(upper, shard - 1 - hop, shard + 1 + hop)
 
-    @pl.loop(0, (nshard - 1) * chunks)
+    @pl.loop(0, steps)
     def _(step):
+        @pl.when(step + lead < steps)
+        def _():
+            advance(step + lead)
+
         hop, chunk = step // chunks, lax.rem(step, chunks)
         below, over = shard - 1 - hop, shard + 1 + hop
-
-        @pl.when(below >= 0)
-        def _():
-            basis_copy(0, below, chunk, False).wait_recv()
-
-            @pl.when(shard < nshard - 1)
-            def _():
-                basis_copy(0, below, chunk, False).start()
-
-        @pl.when(over < nshard)
-        def _():
-            basis_copy(1, over, chunk, False).wait_recv()
-
-            @pl.when(shard > 0)
-            def _():
-                basis_copy(1, over, chunk, False).start()
-
         late = hop - both
 
         @pl.when((late < 0) | ((late < nshard - 1 - 2 * both) & (lax.rem(late + 2 * nshard, 2) == 0)))

time: 67.8 us -> 64.4 us (0.950)
  Pallas kernels: 64.4 us -> 61 us
    pallas_call x1, Pallas kernels: 64.4 us -> 61 us  [per_device(): pl.pallas_call(functools.partial(kernel, nsplit, nshard, nb, pad, chunks,...]
where the time goes in v2:
time: 64.4 us; the launch traced here: 64.2 us
  Pallas kernels  61 us (95%)
  local copies, waits for them, and re-layouts  2.62 us (4%)
  between operations  0.65 us (1%)
    pallas_call x1, Pallas kernels, per_device(): pl.pallas_call(functools.partial(kernel, nsplit, nshard, nb, pad, chunks,...  61 us
    unnamed x4, local copies, waits for them, and re-layouts  2.62 us

profile of v2, /device:TPU:0, one launch (start us, length us, event | category | flops | bytes accessed | tf_op | source)
XLA Modules:
  0.0 64.2 jit_solution(15797827896919312834)
XLA Ops:
  0.6 61.0 %shard_map.50 = (f32[512,2048]{1,0:T(8,128)S(1)}, f32[16,128]{1,0:T(8,128)}) custom-call(bf16[3,128]{1,0:T(4,128)(2,1)} %strain_ref.1, bf16[100,2048]{1,0:T(8,128)(2,1)} %bitcast.8, bf16[2,400,512]{2,1,0:T(8,128)(2,1)} %bitcast.7), custom_call_target="tpu_custom_call" | custom-call | tf_op jit(solution)/shard_map/pallas_call | solution.py:283
  61.6 0.0 copy-start
  61.6 2.0 %copy.7 = f32[1,512,2048]{2,1,0:T(8,128)} copy(f32[1,512,2048]{2,1,0:T(8,128)S(1)} %bitcast.6) | data formatting | bytes 8388608
  63.6 0.0 copy-done
  63.6 0.6 copy.8
Async XLA Ops:
  61.6 2.0 %copy-start = (f32[16,128]{1,0:T(8,128)S(1)}, f32[16,128]{1,0:T(8,128)}, u32[]{:S(2)}) copy-start(f32[16,128]{1,0:T(8,128)} %get-tuple-element.5) | copy-start | bytes 24580

commit v3 on v2

--- a/solution.py
+++ b/solution.py
@@ -15,7 +15,7 @@
     nsplit, nshard, nb, pad, chunks, mtile, scale,
     strain_ref, basis_ref, recon_ref,
     snr_ref, loud_ref,
-    parts, rows, tiles, held, pair, acc, series, weights, localmax, splitmax, shardmax,
+    parts, rows, tiles, held, pair, turned, acc, series, weights, localmax, splitmax, shardmax,
     strain_send, strain_recv, wide_send, wide_recv,
     basis_send, basis_recv, smax_send, smax_recv, hmax_send, hmax_recv,
 ):
@@ -99,10 +99,8 @@
     for off in range(1, nsplit):
         wide_copy(off).wait_recv()
 
-    steps = (nshard - 1) * chunks
     middle = (shard > 0) & (shard < nshard - 1)
-    ahead = chunks - 1
-    lead = jnp.where(middle, ahead, 0)
+    ahead = min(2, chunks)
 
     def advance(step):
         hop, chunk = step // chunks, lax.rem(step, chunks)
@@ -126,7 +124,7 @@
 
     @pl.when(middle)
     def _():
-        for step in range(ahead - 1):
+        for step in range(ahead):
             advance(jnp.int32(step))
 
     per = LANES // width
@@ -154,15 +152,41 @@
 
     lax.fori_loop(1, nrows, tile_step, rolled(jnp.int32(0)))
 
-    @pl.when(middle)
-    def _():
-        advance(jnp.int32(ahead - 1))
-
-    def fir(first, second, chunk):
+    @pl.loop(jnp.where(middle, ahead, 0), chunks)
+    def _(step):
+        advance(step)
+
+    def place(first, second, chunk):
         at_taps = pl.ds(pl.multiple_of(chunk * ctaps, ctaps), ctaps)
         pair[:nb, :] = held[first, :, at_taps]
         pair[pad : pad + nb, :] = held[second, :, at_taps]
-        per_det = tout // mtile
+        turned[at_taps, :] = pair[...].T
+
+    def keep(det, at, first, second, total):
+        series[det, at, pl.ds(pl.multiple_of(first * pad, pad), pad)] = total[:, :pad].astype(jnp.bfloat16)
+        series[det, at, pl.ds(pl.multiple_of(second * pad, pad), pad)] = total[:, pad:].astype(jnp.bfloat16)
+
+    per_det = tout // mtile
+
+    def fir_whole(first, second, beside):
+        @pl.loop(0, chunks)
+        def _(chunk):
+            place(first, second, chunk)
+
+        @pl.loop(0, ndet * per_det)
+        def _(step):
+            det = step // per_det
+            begin = lax.rem(step, per_det) * mtile
+            frame = jnp.concatenate([
+                tiles[det, pl.ds(pl.multiple_of(begin + (ktiles - 1 - i) * LANES, LANES), mtile), :]
+                for i in range(ktiles)], axis=1)
+            at = pl.ds(pl.multiple_of(begin, mtile), mtile)
+            keep(det, at, first, second, jnp.dot(frame, turned[...], preferred_element_type=jnp.float32))
+            beside(step)
+
+    def fir_part(first, second, chunk):
+        place(first, second, chunk)
+        at_taps = pl.ds(pl.multiple_of(chunk * ctaps, ctaps), ctaps)
 
         @pl.loop(0, ndet * per_det)
         def _(step):
@@ -172,14 +196,16 @@
                 tiles[det, pl.ds(pl.multiple_of(begin + (ktiles - 1 - i) * LANES - chunk * ctaps, LANES), mtile), :]
                 for i in range(ctaps // LANES)], axis=1)
             at = pl.ds(pl.multiple_of(begin, mtile), mtile)
-            total = lax.dot_general(frame, pair[...], (((1,), (1,)), ((), ())), preferred_element_type=jnp.float32)
+            total = jnp.dot(frame, turned[at_taps, :], preferred_element_type=jnp.float32)
             total = jnp.where(chunk > 0, acc[det, at, :], 0.0) + total
-            acc[det, at, :] = total
+
+            @pl.when(chunk < chunks - 1)
+            def _():
+                acc[det, at, :] = total
 
             @pl.when(chunk == chunks - 1)
             def _():
-                series[det, at, pl.ds(pl.multiple_of(first * pad, pad), pad)] = total[:, :pad].astype(jnp.bfloat16)
-                series[det, at, pl.ds(pl.multiple_of(second * pad, pad), pad)] = total[:, pad:].astype(jnp.bfloat16)
+                keep(det, at, first, second, total)
 
     both = jnp.minimum(shard, nshard - 1 - shard)
     upper = shard >= nshard // 2
@@ -187,21 +213,39 @@
     def single(hop):
         return jnp.where(upper, shard - 1 - hop, shard + 1 + hop)
 
-    @pl.loop(0, steps)
-    def _(step):
-        @pl.when(step + lead < steps)
-        def _():
-            advance(step + lead)
-
-        hop, chunk = step // chunks, lax.rem(step, chunks)
-        below, over = shard - 1 - hop, shard + 1 + hop
+    @pl.loop(0, nshard - 1)
+    def _(hop):
         late = hop - both
-
-        @pl.when((late < 0) | ((late < nshard - 1 - 2 * both) & (lax.rem(late + 2 * nshard, 2) == 0)))
-        def _():
-            first = jnp.where(late < 0, below, jnp.where(late == 0, shard, single(hop - 1)))
-            second = jnp.where(late < 0, over, single(hop))
-            fir(first, second, chunk)
+        paired = (late < 0) | ((late < nshard - 1 - 2 * both) & (lax.rem(late + 2 * nshard, 2) == 0))
+        first = jnp.where(late < 0, shard - 1 - hop, jnp.where(late == 0, shard, single(hop - 1)))
+        second = jnp.where(late < 0, shard + 1 + hop, single(hop))
+        by_chunk = jnp.logical_not(middle) & (hop == nshard - 2)
+        onward = (hop + 1 < nshard - 1) & (middle | (hop + 1 < nshard - 2))
+
+        @pl.when(by_chunk)
+        def _():
+            @pl.loop(0, chunks)
+            def _(chunk):
+                @pl.when(hop > 0)
+                def _():
+                    advance(hop * chunks + chunk)
+
+                fir_part(first, second, chunk)
+
+        def beside(step):
+            @pl.when(onward & (step < chunks))
+            def _():
+                advance((hop + 1) * chunks + step)
+
+        @pl.when(paired & jnp.logical_not(by_chunk))
+        def _():
+            fir_whole(first, second, beside)
+
+        @pl.when(jnp.logical_not(paired))
+        def _():
+            @pl.loop(0, chunks)
+            def _(step):
+                beside(step)
 
     rtile = 256
 
@@ -294,6 +338,7 @@
             pltpu.VMEM((ndet, taps + tout - LANES, LANES), jnp.bfloat16),
             pltpu.VMEM((nshard, nb, taps), jnp.bfloat16),
             pltpu.VMEM((2 * pad, taps // chunks), jnp.bfloat16),
+            pltpu.VMEM((taps, 2 * pad), jnp.bfloat16),
             pltpu.VMEM((ndet, tout, 2 * pad), jnp.float32),
             pltpu.VMEM((ndet, tout, nshard * pad), jnp.bfloat16),
             pltpu.VMEM((2 * templ, nshard * pad), jnp.bfloat16),

time: 64.4 us -> 63.1 us (0.980)
  Pallas kernels: 61 us -> 59.7 us
    pallas_call x1, Pallas kernels: 61 us -> 59.7 us  [per_device(): pl.pallas_call(functools.partial(kernel, nsplit, nshard, nb, pad, chunks,...]
where the time goes in v3:
time: 63.1 us; the launch traced here: 62.9 us
  Pallas kernels  59.7 us (95%)
  local copies, waits for them, and re-layouts  2.62 us (4%)
  between operations  0.65 us (1%)
    pallas_call x1, Pallas kernels, per_device(): pl.pallas_call(functools.partial(kernel, nsplit, nshard, nb, pad, chunks,...  59.7 us
    unnamed x4, local copies, waits for them, and re-layouts  2.62 us

profile of v3, /device:TPU:0, one launch (start us, length us, event | category | flops | bytes accessed | tf_op | source)
XLA Modules:
  0.0 62.9 jit_solution(16162821261456924933)
XLA Ops:
  0.6 59.7 %shard_map.50 = (f32[512,2048]{1,0:T(8,128)S(1)}, f32[16,128]{1,0:T(8,128)}) custom-call(bf16[3,128]{1,0:T(4,128)(2,1)} %strain_ref.1, bf16[100,2048]{1,0:T(8,128)(2,1)} %bitcast.8, bf16[2,400,512]{2,1,0:T(8,128)(2,1)} %bitcast.7), custom_call_target="tpu_custom_call" | custom-call | tf_op jit(solution)/shard_map/pallas_call | solution.py:327
  60.3 0.0 copy-start
  60.3 2.0 %copy.7 = f32[1,512,2048]{2,1,0:T(8,128)} copy(f32[1,512,2048]{2,1,0:T(8,128)S(1)} %bitcast.6) | data formatting | bytes 8388608
  62.3 0.0 copy-done
  62.3 0.6 copy.8
Async XLA Ops:
  60.3 2.0 %copy-start = (f32[16,128]{1,0:T(8,128)S(1)}, f32[16,128]{1,0:T(8,128)}, u32[]{:S(2)}) copy-start(f32[16,128]{1,0:T(8,128)} %get-tuple-element.5) | copy-start | bytes 24580

commit v4 on v3

--- a/solution.py
+++ b/solution.py
@@ -15,7 +15,7 @@
     nsplit, nshard, nb, pad, chunks, mtile, scale,
     strain_ref, basis_ref, recon_ref,
     snr_ref, loud_ref,
-    parts, rows, tiles, held, pair, turned, acc, series, weights, localmax, splitmax, shardmax,
+    parts, rows, tiles, held, pair, turned, acc, series, partial, weights, localmax, splitmax, shardmax,
     strain_send, strain_recv, wide_send, wide_recv,
     basis_send, basis_recv, smax_send, smax_recv, hmax_send, hmax_recv,
 ):
@@ -162,9 +162,29 @@
         pair[pad : pad + nb, :] = held[second, :, at_taps]
         turned[at_taps, :] = pair[...].T
 
-    def keep(det, at, first, second, total):
-        series[det, at, pl.ds(pl.multiple_of(first * pad, pad), pad)] = total[:, :pad].astype(jnp.bfloat16)
-        series[det, at, pl.ds(pl.multiple_of(second * pad, pad), pad)] = total[:, pad:].astype(jnp.bfloat16)
+    rtile = 256
+
+    def columns(block):
+        return weights[:, pl.ds(pl.multiple_of(block * pad, pad), pad)]
+
+    def term(first, second, det, at):
+        return lax.dot_general(
+            jnp.concatenate([columns(first), columns(second)], axis=1), series[det, at, :],
+            (((1,), (1,)), ((), ())), preferred_element_type=jnp.float32)
+
+    def add_terms(first, second, begins):
+        @pl.loop(0, ndet * (tout // rtile))
+        def _(step):
+            det = step // (tout // rtile)
+            at = pl.ds(pl.multiple_of(lax.rem(step, tout // rtile) * rtile, rtile), rtile)
+
+            @pl.when(begins)
+            def _():
+                partial[det, :, at] = term(first, second, det, at)
+
+            @pl.when(jnp.logical_not(begins))
+            def _():
+                partial[det, :, at] += term(first, second, det, at)
 
     per_det = tout // mtile
 
@@ -181,7 +201,7 @@
                 tiles[det, pl.ds(pl.multiple_of(begin + (ktiles - 1 - i) * LANES, LANES), mtile), :]
                 for i in range(ktiles)], axis=1)
             at = pl.ds(pl.multiple_of(begin, mtile), mtile)
-            keep(det, at, first, second, jnp.dot(frame, turned[...], preferred_element_type=jnp.float32))
+            series[det, at, :] = jnp.dot(frame, turned[...], preferred_element_type=jnp.float32).astype(jnp.bfloat16)
             beside(step)
 
     def fir_part(first, second, chunk):
@@ -205,7 +225,7 @@
 
             @pl.when(chunk == chunks - 1)
             def _():
-                keep(det, at, first, second, total)
+                series[det, at, :] = total.astype(jnp.bfloat16)
 
     both = jnp.minimum(shard, nshard - 1 - shard)
     upper = shard >= nshard // 2
@@ -220,7 +240,12 @@
         first = jnp.where(late < 0, shard - 1 - hop, jnp.where(late == 0, shard, single(hop - 1)))
         second = jnp.where(late < 0, shard + 1 + hop, single(hop))
         by_chunk = jnp.logical_not(middle) & (hop == nshard - 2)
-        onward = (hop + 1 < nshard - 1) & (middle | (hop + 1 < nshard - 2))
+
+        @pl.when(jnp.logical_not(middle) & (hop > 0) & jnp.logical_not(by_chunk))
+        def _():
+            @pl.loop(0, chunks)
+            def _(step):
+                advance(hop * chunks + step)
 
         @pl.when(by_chunk)
         def _():
@@ -233,13 +258,17 @@
                 fir_part(first, second, chunk)
 
         def beside(step):
-            @pl.when(onward & (step < chunks))
+            @pl.when(middle & (hop + 1 < nshard - 1) & (step < chunks))
             def _():
                 advance((hop + 1) * chunks + step)
 
         @pl.when(paired & jnp.logical_not(by_chunk))
         def _():
             fir_whole(first, second, beside)
+
+            @pl.when(hop < nshard - 2 - both)
+            def _():
+                add_terms(first, second, hop == 0)
 
         @pl.when(jnp.logical_not(paired))
         def _():
@@ -247,15 +276,16 @@
             def _(step):
                 beside(step)
 
-    rtile = 256
+    last = nshard - 2 - both
+    first = jnp.where(last == both, shard, single(last - 1))
+    second = single(last)
 
     @pl.loop(0, tout // rtile)
     def _(step):
         at = pl.ds(pl.multiple_of(step * rtile, rtile), rtile)
         total = None
         for det in range(ndet):
-            z = lax.dot_general(
-                weights[...], series[det, at, :], (((1,), (1,)), ((), ())), preferred_element_type=jnp.float32)
+            z = partial[det, :, at] + term(first, second, det, at)
             z = z * z
             z = z[:templ] + z[templ:]
             total = z if total is None else total + z
@@ -340,7 +370,8 @@
             pltpu.VMEM((2 * pad, taps // chunks), jnp.bfloat16),
             pltpu.VMEM((taps, 2 * pad), jnp.bfloat16),
             pltpu.VMEM((ndet, tout, 2 * pad), jnp.float32),
-            pltpu.VMEM((ndet, tout, nshard * pad), jnp.bfloat16),
+            pltpu.VMEM((ndet, tout, 2 * pad), jnp.bfloat16),
+            pltpu.VMEM((ndet, 2 * templ, tout), jnp.float32),
             pltpu.VMEM((2 * templ, nshard * pad), jnp.bfloat16),
             pltpu.VMEM((tout // LANES, LANES), jnp.float32),
             pltpu.VMEM((nsplit - 1, tout // LANES, LANES), jnp.float32),

time: 63.1 us -> 66.5 us (1.054)
  Pallas kernels: 59.7 us -> 63.1 us
    pallas_call x1, Pallas kernels: 59.7 us -> 63.1 us  [per_device(): pl.pallas_call(functools.partial(kernel, nsplit, nshard, nb, pad, chunks,...]
where the time goes in v4:
time: 66.5 us; the launch traced here: 66.4 us
  Pallas kernels  63.1 us (95%)
  local copies, waits for them, and re-layouts  2.62 us (4%)
    pallas_call x1, Pallas kernels, per_device(): pl.pallas_call(functools.partial(kernel, nsplit, nshard, nb, pad, chunks,...  63.1 us
    unnamed x4, local copies, waits for them, and re-layouts  2.62 us

profile of v4, /device:TPU:0, one launch (start us, length us, event | category | flops | bytes accessed | tf_op | source)
XLA Modules:
  0.0 66.4 jit_solution(12766875604355475349)
XLA Ops:
  0.6 63.1 %shard_map.50 = (f32[512,2048]{1,0:T(8,128)S(1)}, f32[16,128]{1,0:T(8,128)}) custom-call(bf16[3,128]{1,0:T(4,128)(2,1)} %strain_ref.1, bf16[100,2048]{1,0:T(8,128)(2,1)} %bitcast.8, bf16[2,400,512]{2,1,0:T(8,128)(2,1)} %bitcast.7), custom_call_target="tpu_custom_call" | custom-call | tf_op jit(solution)/shard_map/pallas_call | solution.py:357
  63.7 0.0 copy-start
  63.8 2.0 %copy.7 = f32[1,512,2048]{2,1,0:T(8,128)} copy(f32[1,512,2048]{2,1,0:T(8,128)S(1)} %bitcast.6) | data formatting | bytes 8388608
  65.8 0.0 copy-done
  65.8 0.6 copy.8
Async XLA Ops:
  63.7 2.0 %copy-start = (f32[16,128]{1,0:T(8,128)S(1)}, f32[16,128]{1,0:T(8,128)}, u32[]{:S(2)}) copy-start(f32[16,128]{1,0:T(8,128)} %get-tuple-element.5) | copy-start | bytes 24580

commit v5 on v3

--- a/solution.py
+++ b/solution.py
@@ -81,7 +81,8 @@
     within = lax.rem(lcol, pad)
     chosen = (lrow == (lcol - within) // pad * nb + within) & (within < nb)
     select = jnp.where(chosen, 1.0, 0.0).astype(jnp.bfloat16)
-    for q in range(2):
+
+    def place_weights(q):
         @pl.loop(0, templ // 256)
         def _(part):
             begin = pl.multiple_of(part * 256, 256)
@@ -89,6 +90,8 @@
                 recon_ref[q, :, pl.ds(begin, 256)], select, (((0,), (0,)), ((), ())),
                 preferred_element_type=jnp.float32)
             weights[pl.ds(pl.multiple_of(q * templ + begin, 256), 256), :] = placed.astype(jnp.bfloat16)
+
+    place_weights(0)
     pair[...] = jnp.zeros_like(pair)
 
     for off in range(1, nshard):
@@ -96,11 +99,11 @@
     for off in range(1, nsplit):
         wide_copy(off).start()
 
+    place_weights(1)
     for off in range(1, nsplit):
         wide_copy(off).wait_recv()
 
     middle = (shard > 0) & (shard < nshard - 1)
-    ahead = min(2, chunks)
 
     def advance(step):
         hop, chunk = step // chunks, lax.rem(step, chunks)
@@ -121,38 +124,40 @@
             @pl.when(shard > 0)
             def _():
                 basis_copy(1, over, chunk, False).start()
-
-    @pl.when(middle)
-    def _():
-        for step in range(ahead):
-            advance(jnp.int32(step))
 
     per = LANES // width
     if per > 1:
         for piece in range(nsplit * nshard):
             rows[piece // per, :, (piece % per) * width : (piece % per + 1) * width] = parts[piece // nshard, piece % nshard]
 
+    else:
+        rows[...] = parts[...].reshape(rows.shape)
+    lane = lax.broadcasted_iota(jnp.int32, (LANES, LANES), 1)
+    line = lax.broadcasted_iota(jnp.int32, (LANES, LANES), 0)
+    mirror = jnp.where(lane + line == LANES - 1, 1.0, 0.0).astype(jnp.bfloat16)
+    rows[...] = jnp.dot(
+        rows[...].reshape(nrows * 8, LANES).astype(jnp.bfloat16), mirror,
+        preferred_element_type=jnp.float32).reshape(rows.shape)
+
     def rolled(b):
-        if per > 1:
-            block = rows[b]
-        else:
-            block = parts[b // nshard, lax.rem(b, nshard)]
+        block = rows[b]
         return tuple(
-            pltpu.roll(jnp.broadcast_to(block[d : d + 1, :], (LANES, LANES)), 1, 1, stride=1, stride_axis=0)
+            pltpu.roll(jnp.broadcast_to(block[d : d + 1, :], (LANES, LANES)), 0, 1, stride=1, stride_axis=0)
             for d in range(ndet))
 
-    above = lax.broadcasted_iota(jnp.int32, (LANES, LANES), 1) > lax.broadcasted_iota(jnp.int32, (LANES, LANES), 0)
-
-    def tile_step(b, last):
-        now = rolled(b)
-        at = pl.ds(pl.multiple_of((b - 1) * LANES, LANES), LANES)
-        for d in range(ndet):
-            tiles[d, at, :] = jnp.where(above, now[d], last[d]).T.astype(jnp.bfloat16)
-        return now
-
-    lax.fori_loop(1, nrows, tile_step, rolled(jnp.int32(0)))
-
-    @pl.loop(jnp.where(middle, ahead, 0), chunks)
+    def tile_step(group, last):
+        for i in range(4):
+            b = group * 4 + i
+            now = rolled(jnp.minimum(b + 1, nrows - 1))
+            at = pl.ds(pl.multiple_of(b * LANES, LANES), LANES)
+            for d in range(ndet):
+                tiles[d, at, :] = jnp.where(lane >= line, last[d], now[d]).astype(jnp.bfloat16)
+            last = now
+        return last
+
+    lax.fori_loop(0, nrows // 4, tile_step, rolled(jnp.int32(0)))
+
+    @pl.loop(0, chunks)
     def _(step):
         advance(step)
 
@@ -220,7 +225,12 @@
         first = jnp.where(late < 0, shard - 1 - hop, jnp.where(late == 0, shard, single(hop - 1)))
         second = jnp.where(late < 0, shard + 1 + hop, single(hop))
         by_chunk = jnp.logical_not(middle) & (hop == nshard - 2)
-        onward = (hop + 1 < nshard - 1) & (middle | (hop + 1 < nshard - 2))
+
+        @pl.when(jnp.logical_not(middle) & (hop > 0) & jnp.logical_not(by_chunk))
+        def _():
+            @pl.loop(0, chunks)
+            def _(step):
+                advance(hop * chunks + step)
 
         @pl.when(by_chunk)
         def _():
@@ -233,7 +243,7 @@
                 fir_part(first, second, chunk)
 
         def beside(step):
-            @pl.when(onward & (step < chunks))
+            @pl.when(middle & (hop + 1 < nshard - 1) & (step < chunks))
             def _():
                 advance((hop + 1) * chunks + step)
 
@@ -321,7 +331,7 @@
     tout = width * nsplit * nshard - taps
     pad = -(-nb // LANES) * LANES
     chunks = 4
-    mtile = 1024
+    mtile = 512
     vmem = pl.BlockSpec(memory_space=pltpu.VMEM)
     dma = pltpu.SemaphoreType.DMA
     snr, loud = pl.pallas_call(
@@ -335,7 +345,7 @@
         scratch_shapes=[
             pltpu.VMEM((nsplit, nshard, 8, width), jnp.float32),
             pltpu.VMEM(((taps + tout) // LANES, 8, LANES), jnp.float32),
-            pltpu.VMEM((ndet, taps + tout - LANES, LANES), jnp.bfloat16),
+            pltpu.VMEM((ndet, taps + tout, LANES), jnp.bfloat16),
             pltpu.VMEM((nshard, nb, taps), jnp.bfloat16),
             pltpu.VMEM((2 * pad, taps // chunks), jnp.bfloat16),
             pltpu.VMEM((taps, 2 * pad), jnp.bfloat16),

time: 63.1 us -> 65.7 us (1.041)
  Pallas kernels: 59.7 us -> 62.3 us
    pallas_call x1, Pallas kernels: 59.7 us -> 62.3 us  [per_device(): pl.pallas_call(functools.partial(kernel, nsplit, nshard, nb, pad, chunks,...]
where the time goes in v5:
time: 65.7 us; the launch traced here: 65.5 us
  Pallas kernels  62.3 us (95%)
  local copies, waits for them, and re-layouts  2.62 us (4%)
    pallas_call x1, Pallas kernels, per_device(): pl.pallas_call(functools.partial(kernel, nsplit, nshard, nb, pad, chunks,...  62.3 us
    unnamed x4, local copies, waits for them, and re-layouts  2.62 us

profile of v5, /device:TPU:0, one launch (start us, length us, event | category | flops | bytes accessed | tf_op | source)
XLA Modules:
  0.0 65.5 jit_solution(6788912076231228992)
XLA Ops:
  0.6 62.3 %shard_map.50 = (f32[512,2048]{1,0:T(8,128)S(1)}, f32[16,128]{1,0:T(8,128)}) custom-call(bf16[3,128]{1,0:T(4,128)(2,1)} %strain_ref.1, bf16[100,2048]{1,0:T(8,128)(2,1)} %bitcast.8, bf16[2,400,512]{2,1,0:T(8,128)(2,1)} %bitcast.7), custom_call_target="tpu_custom_call" | custom-call | tf_op jit(solution)/shard_map/pallas_call | solution.py:337
  62.9 0.0 copy-start
  62.9 2.0 %copy.7 = f32[1,512,2048]{2,1,0:T(8,128)} copy(f32[1,512,2048]{2,1,0:T(8,128)S(1)} %bitcast.6) | data formatting | bytes 8388608
  64.9 0.0 copy-done
  64.9 0.6 copy.8
Async XLA Ops:
  62.9 2.0 %copy-start = (f32[16,128]{1,0:T(8,128)S(1)}, f32[16,128]{1,0:T(8,128)}, u32[]{:S(2)}) copy-start(f32[16,128]{1,0:T(8,128)} %get-tuple-element.5) | copy-start | bytes 24580

commit v6 on v5

--- a/solution.py
+++ b/solution.py
@@ -125,6 +125,13 @@
             def _():
                 basis_copy(1, over, chunk, False).start()
 
+    ahead = min(2, chunks)
+
+    @pl.when(middle)
+    def _():
+        for step in range(ahead):
+            advance(jnp.int32(step))
+
     per = LANES // width
     if per > 1:
         for piece in range(nsplit * nshard):
@@ -157,7 +164,7 @@
 
     lax.fori_loop(0, nrows // 4, tile_step, rolled(jnp.int32(0)))
 
-    @pl.loop(0, chunks)
+    @pl.loop(jnp.where(middle, ahead, 0), chunks)
     def _(step):
         advance(step)
 
@@ -331,7 +338,7 @@
     tout = width * nsplit * nshard - taps
     pad = -(-nb // LANES) * LANES
     chunks = 4
-    mtile = 512
+    mtile = 1024
     vmem = pl.BlockSpec(memory_space=pltpu.VMEM)
     dma = pltpu.SemaphoreType.DMA
     snr, loud = pl.pallas_call(

time: 65.7 us -> 62.5 us (0.951)
  Pallas kernels: 62.3 us -> 59.1 us
    pallas_call x1, Pallas kernels: 62.3 us -> 59.1 us  [per_device(): pl.pallas_call(functools.partial(kernel, nsplit, nshard, nb, pad, chunks,...]
where the time goes in v6:
time: 62.5 us; the launch traced here: 62.4 us
  Pallas kernels  59.1 us (95%)
  local copies, waits for them, and re-layouts  2.62 us (4%)
  between operations  0.65 us (1%)
    pallas_call x1, Pallas kernels, per_device(): pl.pallas_call(functools.partial(kernel, nsplit, nshard, nb, pad, chunks,...  59.1 us
    unnamed x4, local copies, waits for them, and re-layouts  2.62 us

profile of v6, /device:TPU:0, one launch (start us, length us, event | category | flops | bytes accessed | tf_op | source)
XLA Modules:
  0.0 62.4 jit_solution(12760592185690238454)
XLA Ops:
  0.6 59.1 %shard_map.50 = (f32[512,2048]{1,0:T(8,128)S(1)}, f32[16,128]{1,0:T(8,128)}) custom-call(bf16[3,128]{1,0:T(4,128)(2,1)} %strain_ref.1, bf16[100,2048]{1,0:T(8,128)(2,1)} %bitcast.8, bf16[2,400,512]{2,1,0:T(8,128)(2,1)} %bitcast.7), custom_call_target="tpu_custom_call" | custom-call | tf_op jit(solution)/shard_map/pallas_call | solution.py:344
  59.7 0.0 copy-start
  59.7 2.0 %copy.7 = f32[1,512,2048]{2,1,0:T(8,128)} copy(f32[1,512,2048]{2,1,0:T(8,128)S(1)} %bitcast.6) | data formatting | bytes 8388608
  61.8 0.0 copy-done
  61.8 0.6 copy.8
Async XLA Ops:
  59.7 2.0 %copy-start = (f32[16,128]{1,0:T(8,128)S(1)}, f32[16,128]{1,0:T(8,128)}, u32[]{:S(2)}) copy-start(f32[16,128]{1,0:T(8,128)} %get-tuple-element.5) | copy-start | bytes 24580

commit v7 on v6

--- a/solution.py
+++ b/solution.py
@@ -180,21 +180,26 @@
 
     per_det = tout // mtile
 
+    wtile = min(2 * mtile, tout)
+    per_whole = tout // wtile
+    span = -(-chunks // (ndet * per_whole))
+
     def fir_whole(first, second, beside):
         @pl.loop(0, chunks)
         def _(chunk):
             place(first, second, chunk)
 
-        @pl.loop(0, ndet * per_det)
+        @pl.loop(0, ndet * per_whole)
         def _(step):
-            det = step // per_det
-            begin = lax.rem(step, per_det) * mtile
+            det = step // per_whole
+            begin = lax.rem(step, per_whole) * wtile
             frame = jnp.concatenate([
-                tiles[det, pl.ds(pl.multiple_of(begin + (ktiles - 1 - i) * LANES, LANES), mtile), :]
+                tiles[det, pl.ds(pl.multiple_of(begin + (ktiles - 1 - i) * LANES, LANES), wtile), :]
                 for i in range(ktiles)], axis=1)
-            at = pl.ds(pl.multiple_of(begin, mtile), mtile)
+            at = pl.ds(pl.multiple_of(begin, wtile), wtile)
             keep(det, at, first, second, jnp.dot(frame, turned[...], preferred_element_type=jnp.float32))
-            beside(step)
+            for i in range(span):
+                beside(step * span + i)
 
     def fir_part(first, second, chunk):
         place(first, second, chunk)

time: 62.5 us -> 62.5 us (level)
  no operation moved by 1% of the time
where the time goes in v7:
time: 62.5 us; the launch traced here: 62.4 us
  Pallas kernels  59.1 us (95%)
  local copies, waits for them, and re-layouts  2.62 us (4%)
  between operations  0.65 us (1%)
    pallas_call x1, Pallas kernels, per_device(): pl.pallas_call(functools.partial(kernel, nsplit, nshard, nb, pad, chunks,...  59.1 us
    unnamed x4, local copies, waits for them, and re-layouts  2.62 us

profile of v7, /device:TPU:0, one launch (start us, length us, event | category | flops | bytes accessed | tf_op | source)
XLA Modules:
  0.0 62.4 jit_solution(4084930406093051059)
XLA Ops:
  0.6 59.1 %shard_map.50 = (f32[512,2048]{1,0:T(8,128)S(1)}, f32[16,128]{1,0:T(8,128)}) custom-call(bf16[3,128]{1,0:T(4,128)(2,1)} %strain_ref.1, bf16[100,2048]{1,0:T(8,128)(2,1)} %bitcast.8, bf16[2,400,512]{2,1,0:T(8,128)(2,1)} %bitcast.7), custom_call_target="tpu_custom_call" | custom-call | tf_op jit(solution)/shard_map/pallas_call | solution.py:349
  59.7 0.0 copy-start
  59.7 2.0 %copy.7 = f32[1,512,2048]{2,1,0:T(8,128)} copy(f32[1,512,2048]{2,1,0:T(8,128)S(1)} %bitcast.6) | data formatting | bytes 8388608
  61.8 0.0 copy-done
  61.8 0.6 copy.8
Async XLA Ops:
  59.7 2.0 %copy-start = (f32[16,128]{1,0:T(8,128)S(1)}, f32[16,128]{1,0:T(8,128)}, u32[]{:S(2)}) copy-start(f32[16,128]{1,0:T(8,128)} %get-tuple-element.5) | copy-start | bytes 24580
